TPU v7x, 32 devices: a whole 2x2x4 slice. The times are simulated.
32 devices in a mesh: section: 2 (over y), tp: 16 (over z, x, core).
Axes of the slice: x: 2, y: 2, z: 4, core: 2. Of those that a mesh axis runs over, the one named last changes fastest.
Arguments:
- hidden_in: bfloat16 [2, 512, 4096], P('section', 'tp'), may hold values from -6 to 6
- attn_gain: float32 [2, 4096], P('section'), may hold values from 0.1 to 1.9
- w_query: bfloat16 [2, 4096, 4096], P('section', None, 'tp'), may hold values from -0.21875 to 0.21875
- w_keyval: bfloat16 [2, 4096, 2048], P('section', None, 'tp'), may hold values from -0.09375 to 0.09375
- w_out: bfloat16 [2, 4096, 4096], P('section', 'tp'), may hold values from -0.75 to 0.75
- cache: bfloat16 [2, 8, 65536, 256], P('section', None, 'tp'), may hold values from -96 to 96
- starts: int32 [2], P('section'), may hold values from 16384 to 65536, as said below
- owners: int32 [2, 8, 2, 4], replicated, may hold values from 0 to 31, as said below
Outputs:
- hidden_out: bfloat16 [2, 512, 4096], P('section', 'tp')
- page_pool: bfloat16 [384, 128, 128], P(('section', 'tp'))
Inputs may be any that keep to these rules, and one draw needn't show every extreme that they name: `starts`: multiples of 128; one of the two equals 65536. `owners`: every device is named at most 12 times in all, and one device exactly 12 times.
All inputs are finite; a program needn't handle non-finite values.
Results may differ from a plain program's by a relative error of at most 0.02.
The roundings to bfloat16 on the way count: a program that leaves them out, or rounds other values in their place, can miss the bound.
Values may be sent and summed in bfloat16 or wider, within the bound.
A program may use at most 192 MiB of HBM per device.

v0:
```python
import math

import jax
import jax.numpy as jnp
from jax import lax
from jax.experimental import pallas as pl
from jax.experimental.pallas import tpu as pltpu
from jax.sharding import PartitionSpec as P

D = 4096
H = 32
KVH = 8
HD = 128
PAGE = 128
DBLOCK = 4
FRESH = 512


def passed_along(block, axis, distance):
    devices = range(lax.axis_size(axis))
    route = [((i - distance) % len(devices), i) for i in devices]
    return lax.ppermute(block, axis, route)


def rms_norm(values, gain_vec):
    return values * lax.rsqrt(jnp.mean(values * values, axis=-1, keepdims=True) + 1e-06) * gain_vec


def rotate(vectors, positions):
    half_dim = vectors.shape[-1] // 2
    freq_index = jnp.arange(half_dim).astype(jnp.float32)
    inv_freq = jnp.exp(freq_index * (-2.0 * math.log(1000000.0) / vectors.shape[-1]))
    angles = positions.astype(jnp.float32)[:, None] * inv_freq[None, :]
    cosine = jnp.cos(angles)[:, None, :]
    sine = jnp.sin(angles)[:, None, :]
    first_half = vectors[..., :half_dim]
    second_half = vectors[..., half_dim:]
    return jnp.concatenate(
        [first_half * cosine - second_half * sine, second_half * cosine + first_half * sine],
        axis=-1,
    )


def pick_pages(page_set, owner_flat, section_slot, target, capacity):
    per_section = page_set.shape[0]
    is_mine = (owner_flat == target).astype(jnp.int32)
    slot_rank = jnp.cumsum(is_mine) - 1
    mine_here = lax.dynamic_slice_in_dim(is_mine, section_slot * per_section, per_section)
    rank_here = lax.dynamic_slice_in_dim(slot_rank, section_slot * per_section, per_section)
    wanted = (mine_here[None, :] == 1) & (rank_here[None, :] == jnp.arange(capacity)[:, None])
    return jnp.einsum(
        "cp,pxd->cxd", wanted.astype(jnp.bfloat16), page_set, preferred_element_type=jnp.float32
    )


def general_body(hidden_in, attn_gain, w_query, w_keyval, w_out, cache, starts, owners):
    tp_count = lax.axis_size("tp")
    section_count = lax.axis_size("section")
    tp_rank = lax.axis_index("tp")
    section_rank = lax.axis_index("section")
    group_size = H // KVH
    local_rows = hidden_in.shape[1]
    query_cols = w_query.shape[2]
    inv_scale = 1.0 / math.sqrt(HD)
    residual = hidden_in[0].astype(jnp.float32)
    normed = rms_norm(residual, attn_gain[0]).astype(jnp.bfloat16)
    query_weight = w_query[0]
    keyval_weight = w_keyval[0]
    rows_piece = lax.all_gather(normed, "tp", axis=0, tiled=True)
    projected = jnp.concatenate(
        [
            jnp.dot(rows_piece, query_weight, preferred_element_type=jnp.float32),
            jnp.dot(rows_piece, keyval_weight, preferred_element_type=jnp.float32),
        ],
        axis=1,
    )
    query_part = projected[:, :query_cols].astype(jnp.bfloat16)
    keyval_part = projected[:, query_cols:].astype(jnp.bfloat16)
    queries, keyval = (
        lax.all_gather(query_part, "tp", axis=1, tiled=True),
        lax.all_gather(keyval_part, "tp", axis=1, tiled=True),
    )
    block_start = starts[0]
    positions = block_start + jnp.arange(FRESH, dtype=jnp.int32)
    q_rot = rotate(queries.reshape(FRESH, H, HD).astype(jnp.float32), positions).astype(
        jnp.bfloat16
    )
    q_rot = q_rot.reshape(FRESH, KVH, group_size, HD)
    split_kv = keyval.reshape(FRESH, KVH, 2, HD)
    k_new = rotate(split_kv[:, :, 0].astype(jnp.float32), positions).astype(jnp.bfloat16)
    v_new = split_kv[:, :, 1]
    slot_count = cache.shape[2]
    fresh_count = FRESH // tp_count
    slot_positions = tp_rank * slot_count + jnp.arange(slot_count, dtype=jnp.int32)
    cached_ok = slot_positions < block_start
    fresh_index = tp_rank * fresh_count + jnp.arange(fresh_count, dtype=jnp.int32)
    row_block = jnp.arange(FRESH, dtype=jnp.int32) // DBLOCK
    fresh_ok = fresh_index[None, :] // DBLOCK <= row_block[:, None]
    fresh_keys = lax.dynamic_slice_in_dim(k_new, tp_rank * fresh_count, fresh_count, 0)
    fresh_vals = lax.dynamic_slice_in_dim(v_new, tp_rank * fresh_count, fresh_count, 0)
    local_cache = cache[0]

    def one_group(group_index, carry):
        tops, totals, sums = carry
        query_group = lax.dynamic_index_in_dim(q_rot, group_index, 1, False)
        cached = lax.dynamic_index_in_dim(local_cache, group_index, 0, False)
        cached_keys = cached[:, :HD]
        cached_vals = cached[:, HD:]
        new_keys = lax.dynamic_index_in_dim(fresh_keys, group_index, 1, False)
        new_vals = lax.dynamic_index_in_dim(fresh_vals, group_index, 1, False)
        cached_scores = (
            jnp.einsum("rqd,kd->rqk", query_group, cached_keys, preferred_element_type=jnp.float32)
            * inv_scale
        )
        new_scores = (
            jnp.einsum("rqd,kd->rqk", query_group, new_keys, preferred_element_type=jnp.float32)
            * inv_scale
        )
        cached_scores = jnp.where(cached_ok[None, None, :], cached_scores, -jnp.inf)
        new_scores = jnp.where(fresh_ok[:, None, :], new_scores, -jnp.inf)
        row_top = jnp.maximum(jnp.max(cached_scores, axis=-1), jnp.max(new_scores, axis=-1))
        shift_by = jnp.where(row_top > -jnp.inf, row_top, 0.0)
        cached_weights = jnp.exp(cached_scores - shift_by[..., None])
        new_weights = jnp.exp(new_scores - shift_by[..., None])
        weight_sum = jnp.sum(cached_weights, axis=-1) + jnp.sum(new_weights, axis=-1)
        value_sum = jnp.einsum(
            "rqk,kd->rqd",
            cached_weights.astype(jnp.bfloat16),
            cached_vals,
            preferred_element_type=jnp.float32,
        )
        value_sum = value_sum + jnp.einsum(
            "rqk,kd->rqd",
            new_weights.astype(jnp.bfloat16),
            new_vals,
            preferred_element_type=jnp.float32,
        )
        tops = lax.dynamic_update_index_in_dim(tops, row_top, group_index, 1)
        totals = lax.dynamic_update_index_in_dim(totals, weight_sum, group_index, 1)
        sums = lax.dynamic_update_index_in_dim(sums, value_sum, group_index, 1)
        return (tops, totals, sums)

    initial = (
        jnp.full((FRESH, KVH, group_size), -jnp.inf, jnp.float32),
        jnp.zeros((FRESH, KVH, group_size), jnp.float32),
        jnp.zeros((FRESH, KVH, group_size, HD), jnp.float32),
    )
    tops, totals, sums = lax.fori_loop(0, KVH, one_group, initial)
    tops = tops.reshape(FRESH, H)
    totals = totals.reshape(FRESH, H)
    peak = lax.pmax(tops.astype(jnp.bfloat16), "tp").astype(tops.dtype)
    factor = jnp.where(tops > -jnp.inf, jnp.exp(tops - peak), 0.0)
    scaled = (sums.reshape(FRESH, H, HD) * factor[:, :, None]).reshape(FRESH, D)
    head_share = lax.psum_scatter(scaled, "tp", scatter_dimension=1, tiled=True)
    weight_total = lax.psum(totals * factor, "tp")
    share_cols = head_share.shape[1]
    heads_here = max(share_cols // HD, 1)
    first_head = tp_rank * share_cols // HD
    denominator = lax.dynamic_slice_in_dim(weight_total, first_head, heads_here, 1)
    attended = (
        head_share.reshape(FRESH, heads_here, share_cols // heads_here) / denominator[:, :, None]
    )
    attended = attended.reshape(FRESH, share_cols).astype(jnp.bfloat16)
    out_weight = w_out[0]
    full_sum = lax.psum(jnp.dot(attended, out_weight, preferred_element_type=jnp.float32), "tp")
    projected_rows = lax.dynamic_slice_in_dim(full_sum, tp_rank * local_rows, local_rows, 0)
    layer_out = (residual + projected_rows).astype(jnp.bfloat16)
    passed_on = passed_along(layer_out, "section", 1)
    stacked = jnp.stack([k_new, v_new], axis=2).reshape(FRESH // PAGE, PAGE, KVH, 2, HD)
    local_pages = jnp.transpose(stacked, (2, 3, 0, 1, 4)).reshape(-1, PAGE, HD)
    owner_flat = owners.reshape(-1)
    capacity = 3 * max(owner_flat.shape[0] // (section_count * tp_count), 1)
    self_index = section_rank * tp_count + tp_rank
    page_slots = pick_pages(local_pages, owner_flat, section_rank, self_index, capacity)
    prior_section = (section_rank + section_count - 1) % section_count
    earlier_pages = passed_along(local_pages, "section", 1)
    page_slots = page_slots + pick_pages(
        earlier_pages, owner_flat, prior_section, self_index, capacity
    )
    return (passed_on[None], page_slots.astype(jnp.bfloat16))


NEG = -1e30
CHUNKS = 2
ROW_TILE = 256
TILES = 4


def attend_kernel(count_ref, q_ref, kv_ref, sums_ref, lse_ref, *, tile, scale):
    slots = kv_ref.shape[1]
    rows = q_ref.shape[1]
    count = count_ref[0]

    def run(masked):
        keys = kv_ref[0, :, :HD]
        vals = kv_ref[0, :, HD:]
        vals_one = jnp.concatenate([vals, jnp.ones_like(vals)], axis=1)
        if masked:
            seen = lax.broadcasted_iota(jnp.int32, (1, slots), 1) < count

        def scores_of(at):
            return lax.dot_general(
                q_ref[0, at * tile : (at + 1) * tile, :],
                keys,
                (((1,), (1,)), ((), ())),
                preferred_element_type=jnp.float32,
            )

        scores = scores_of(0)
        for at in range(rows // tile):
            later = scores_of(at + 1) if at + 1 < rows // tile else None
            if masked:
                scores = jnp.where(seen, scores, NEG)
            top = jnp.max(scores, axis=1, keepdims=True)
            weights = jnp.exp2((scores - top) * scale)
            if masked:
                weights = jnp.where(seen, weights, 0.0)
            both = jnp.dot(
                weights.astype(jnp.bfloat16), vals_one, preferred_element_type=jnp.float32
            )
            total = both[:, HD:]
            safe = jnp.where(total > 0.0, total, 1.0)
            sums_ref[0, at * tile : (at + 1) * tile, :] = both[:, :HD] / safe
            lse = jnp.where(total > 0.0, top * scale + jnp.log2(safe), NEG)
            lse_ref[0, 0:1, at * tile : (at + 1) * tile] = jnp.transpose(lse)[0:1, :]
            scores = later

    @pl.when(count == slots)
    def _():
        run(False)

    @pl.when((count > 0) & (count < slots))
    def _():
        run(True)

    @pl.when(count == 0)
    def _():
        sums_ref[...] = jnp.zeros_like(sums_ref)
        lse_ref[...] = jnp.full_like(lse_ref, NEG)


def attend(q_all, local_cache, count):
    groups, rows, _ = q_all.shape
    slots = local_cache.shape[1]
    tile = min(ROW_TILE, rows)
    block = min(tile * TILES, rows)
    scale = math.log2(math.e) / math.sqrt(HD)
    return pl.pallas_call(
        lambda *refs: attend_kernel(*refs, tile=tile, scale=scale),
        grid_spec=pltpu.PrefetchScalarGridSpec(
            num_scalar_prefetch=1,
            grid=(groups, rows // block),
            in_specs=[
                pl.BlockSpec((1, block, HD), lambda g, r, n: (g, r, 0)),
                pl.BlockSpec((1, slots, 2 * HD), lambda g, r, n: (g, 0, 0)),
            ],
            out_specs=[
                pl.BlockSpec((1, block, HD), lambda g, r, n: (g, r, 0)),
                pl.BlockSpec((1, 1, block), lambda g, r, n: (g, 0, r)),
            ],
        ),
        out_shape=[
            jax.ShapeDtypeStruct((groups, rows, HD), jnp.float32),
            jax.ShapeDtypeStruct((groups, 1, rows), jnp.float32),
        ],
        compiler_params=pltpu.CompilerParams(vmem_limit_bytes=50 * 1024 * 1024),
        cost_estimate=pl.CostEstimate(
            flops=4 * groups * rows * slots * HD,
            bytes_accessed=groups * slots * HD * 4 + groups * rows * HD * 6,
            transcendentals=groups * rows * slots,
        ),
    )(count, q_all, local_cache)


def take_pages(pages, owner_flat, target, capacity):
    mine = owner_flat == target
    rank = jnp.cumsum(mine.astype(jnp.int32)) - 1
    wanted = mine[None, :] & (rank[None, :] == jnp.arange(capacity)[:, None])
    picked = jnp.sum(jnp.where(wanted, jnp.arange(mine.shape[0])[None, :], 0), axis=1)
    filled = jnp.any(wanted, axis=1)
    taken = [lax.dynamic_index_in_dim(pages, picked[k], 0, True) for k in range(capacity)]
    return jnp.where(filled[:, None, None], jnp.concatenate(taken, axis=0), 0)


def body(hidden_in, attn_gain, w_query, w_keyval, w_out, cache, starts, owners):
    query_cols = w_query.shape[2]
    keyval_cols = w_keyval.shape[2]
    if query_cols != 2 * HD or keyval_cols != HD:
        return general_body(
            hidden_in, attn_gain, w_query, w_keyval, w_out, cache, starts, owners
        )
    tp_count = lax.axis_size("tp")
    section_count = lax.axis_size("section")
    tp_rank = lax.axis_index("tp")
    section_rank = lax.axis_index("section")
    local_rows = hidden_in.shape[1]
    heads_here = query_cols // HD
    scale = math.log2(math.e) / math.sqrt(HD)
    residual = hidden_in[0].astype(jnp.float32)
    normed = rms_norm(residual, attn_gain[0]).astype(jnp.bfloat16)
    all_rows = lax.all_gather(normed, "tp", axis=0, tiled=True)
    block_start = starts[0]
    positions = block_start + jnp.arange(FRESH, dtype=jnp.int32)
    queries = jnp.dot(all_rows, w_query[0], preferred_element_type=jnp.float32)
    queries = queries.astype(jnp.bfloat16).astype(jnp.float32)
    q_rot = rotate(queries.reshape(FRESH, heads_here, HD), positions).astype(jnp.bfloat16)
    q_rot = jnp.transpose(q_rot, (1, 0, 2))
    keyval = jnp.dot(all_rows, w_keyval[0], preferred_element_type=jnp.float32)
    keyval = keyval.astype(jnp.bfloat16)
    turned = rotate(keyval.astype(jnp.float32)[:, None, :], positions)[:, 0]
    holds_key = tp_rank % 2 == 0
    part = jnp.where(holds_key, turned.astype(jnp.bfloat16), keyval)
    pair = [(i, i ^ 1) for i in range(tp_count)]
    other = lax.ppermute(part, "tp", pair)
    fresh_key = jnp.where(holds_key, part, other)
    fresh_val = jnp.where(holds_key, other, part)

    step = local_rows // CHUNKS
    by_chunk = q_rot.reshape(heads_here, tp_count, CHUNKS, step, HD)
    part_rows = tp_count * step
    slots = cache.shape[2]
    count = jnp.clip(block_start - tp_rank * slots, 0, slots).reshape(1)
    local_cache = cache[0]
    token = jnp.arange(FRESH, dtype=jnp.int32).reshape(tp_count, CHUNKS, step)
    gathered = [
        lax.all_gather(
            by_chunk[:, :, c].reshape(heads_here, part_rows, HD), "tp", axis=0, tiled=True
        )
        for c in range(CHUNKS)
    ]
    outs = []
    for c in range(CHUNKS):
        q_all = gathered[c].reshape(KVH, H // KVH * part_rows, HD)
        sums, lse = attend(q_all, local_cache, count)
        sums = sums.reshape(H, part_rows, HD)
        lse = lse.reshape(H, part_rows)
        lses = lax.all_gather(lse, "tp", axis=0)
        peak = jnp.max(lses, axis=0)
        whole = peak + jnp.log2(jnp.sum(jnp.exp2(lses - peak[None]), axis=0))
        scaled = sums * jnp.exp2(lse - whole)[:, :, None]
        share = lax.psum_scatter(scaled, "tp", scatter_dimension=0, tiled=True)
        whole_here = lax.dynamic_slice_in_dim(whole, tp_rank * heads_here, heads_here, 0)
        mine = by_chunk[:, :, c].reshape(heads_here, part_rows, HD)
        new_scores = jnp.einsum(
            "hrd,kd->hrk", mine, fresh_key, preferred_element_type=jnp.float32
        )
        row_block = token[:, c].reshape(part_rows) // DBLOCK
        fresh_ok = jnp.arange(FRESH, dtype=jnp.int32)[None, :] // DBLOCK <= row_block[:, None]
        new_scores = jnp.where(fresh_ok[None], new_scores * scale, NEG)
        new_top = jnp.max(new_scores, axis=-1, keepdims=True)
        new_weights = jnp.exp2(new_scores - new_top)
        new_total = jnp.sum(new_weights, axis=-1)
        new_sums = jnp.einsum(
            "hrk,kd->hrd",
            new_weights.astype(jnp.bfloat16),
            fresh_val,
            preferred_element_type=jnp.float32,
        )
        joint = jnp.maximum(new_top[..., 0], whole_here)
        old_part = jnp.exp2(whole_here - joint)
        new_part = jnp.exp2(new_top[..., 0] - joint)
        attended = (share * old_part[..., None] + new_sums * new_part[..., None]) / (
            old_part + new_total * new_part
        )[..., None]
        attended = jnp.transpose(attended.astype(jnp.bfloat16), (1, 0, 2))
        attended = attended.reshape(part_rows, query_cols)
        product = jnp.dot(attended, w_out[0], preferred_element_type=jnp.float32)
        outs.append(lax.psum_scatter(product, "tp", scatter_dimension=0, tiled=True))
    projected_rows = jnp.stack(outs, axis=0).reshape(local_rows, D)
    layer_out = (residual + projected_rows).astype(jnp.bfloat16)
    passed_on = passed_along(layer_out, "section", 1)

    pages = lax.all_gather(part, ("section", "tp"), axis=0, tiled=True)
    pages = pages.reshape(-1, PAGE, HD)
    owner_flat = owners.reshape(-1)
    capacity = 3 * max(owner_flat.shape[0] // (section_count * tp_count), 1)
    self_index = section_rank * tp_count + tp_rank
    return (passed_on[None], take_pages(pages, owner_flat, self_index, capacity))


def solution(mesh):
    in_specs = (
        P("section", "tp", None),
        P("section", None),
        P("section", None, "tp"),
        P("section", None, "tp"),
        P("section", "tp", None),
        P("section", None, "tp", None),
        P("section"),
        P(),
    )
    out_specs = (P("section", "tp", None), P(("section", "tp"), None, None))
    return jax.shard_map(body, mesh=mesh, in_specs=in_specs, out_specs=out_specs, check_vma=False)
```

profile of v0, /device:TPU:0, one launch (start us, length us, event | category | flops | bytes accessed | tf_op | source)
XLA Modules:
  0.0 570.4 jit_solution(16044515411526316091)
XLA Ops:
  7.2 1.2 fusion.22
  8.5 1.8 fusion.24
  11.0 1.8 multiply_cosine_fusion
  12.8 51.2 %all-gather.5.cloned.1.call-done = bf16[512,4096]{1,0:T(8,128)(2,1)} async-done(((bf16[32,4096]{1,0:T(8,128)(2,1)}), bf16[512,4096]{1,0:T(8,128)(2,1)}) %all-gather.5.cloned.1.call-update) | async-done | bytes 4194320 | tf_op jit(solution)/shard_map/all_gather | solution.py:301
  64.0 4.2 fusion.8
  68.7 1.2 subtract_convert_fusion
  71.7 39.1 %all-gather.9.cloned.1.call-done = bf16[32,256,128]{2,1,0:T(8,128)(2,1)} async-done(((bf16[2,256,128]{2,1,0:T(8,128)(2,1)}), bf16[32,256,128]{2,1,0:T(8,128)(2,1)}) %all-gather.9.cloned.1.call-update) | async-done | bytes 2097168 | tf_op jit(solution)/shard_map/all_gather | solution.py:326
  110.8 1.6 copy-done.2
  112.4 42.5 %shard_map.96 = (f32[8,1024,128]{2,1,0:T(8,128)}, f32[8,1,1024]{2,1,0:T(1,128)S(1)}) custom-call(s32[1]{0:T(128)} %bitcast.2.refs_0_, bf16[8,1024,128]{2,1,0:T(8,128)(2,1)S(1)} %bitcast.90, bf16[8,4096,256]{2,1,0:T(8,128)(2,1)} %bitcast.117), custom_call_target="tpu_custom_call" | custom-call | flops 17179869184 | bytes 23068672 | tf_op jit(solution)/shard_map/pallas_call | solution.py:248
  155.1 5.6 copy.77
  160.7 20.8 %all_gather.22 = f32[16,32,256]{2,1,0:T(8,128)S(1)} all-gather(f32[1,32,256]{2,1,0:T(8,128)S(1)} %all_gather_reshape.7), channel_id=1, replica_groups=mesh['section'=2,'tp'=16] {'tp'}, dimensions={0}, use_global_device_ids=true | all-gather | bytes 557056 | tf_op jit(solution)/shard_map/all_gather | solution.py:337
  182.2 4.7 broadcast_multiply_fusion
  187.1 1.6 copy-done.1
  188.6 42.5 %shard_map.95 = (f32[8,1024,128]{2,1,0:T(8,128)}, f32[8,1,1024]{2,1,0:T(1,128)S(1)}) custom-call(s32[1]{0:T(128)} %bitcast.2.refs_0_, bf16[8,1024,128]{2,1,0:T(8,128)(2,1)S(1)} %bitcast.89, bf16[8,4096,256]{2,1,0:T(8,128)(2,1)} %bitcast.118), custom_call_target="tpu_custom_call" | custom-call | flops 17179869184 | bytes 23068672 | tf_op jit(solution)/shard_map/pallas_call | solution.py:248
  231.3 5.7 %copy.75 = f32[32,256,128]{1,2,0:T(8,128)} copy(f32[32,256,128]{2,1,0:T(8,128)} %bitcast.103) | data formatting | bytes 8388608 | tf_op jit(solution)/shard_map/reshape | solution.py:335
  237.0 20.3 %all_gather.20 = f32[16,32,256]{2,1,0:T(8,128)S(1)} all-gather(f32[1,32,256]{2,1,0:T(8,128)S(1)} %all_gather_reshape.6), channel_id=1, replica_groups=mesh['section'=2,'tp'=16] {'tp'}, dimensions={0}, use_global_device_ids=true | all-gather | bytes 557056 | tf_op jit(solution)/shard_map/all_gather | solution.py:337
  258.1 4.7 broadcast_multiply_fusion.1
  262.9 1.1 copy-done.4
  264.0 3.7 bitcast_convert_fusion
  271.0 1.4 fusion.68
  273.4 1.5 fusion.16
  274.9 2.7 fusion
  279.2 59.7 %reduce-scatter.5.cloned.1.call-done = f32[2,256,128]{1,2,0:T(8,128)} async-done(((f32[32,256,128]{1,2,0:T(8,128)}), f32[2,256,128]{1,2,0:T(8,128)}) %reduce-scatter.5.cloned.1.call-update) | async-done | bytes 262160 | tf_op jit(solution)/shard_map/reduce_scatter | solution.py:341
  338.9 1.5 fusion.15
  340.4 2.7 fusion.2
  367.5 37.4 %all-gather.11.cloned.1.call-done = bf16[16384,128]{0,1:T(8,128)(2,1)} async-done(((bf16[512,128]{0,1:T(8,128)(2,1)}), bf16[16384,128]{0,1:T(8,128)(2,1)}) %all-gather.11.cloned.1.call-update) | async-done | bytes 4194320 | tf_op jit(solution)/shard_map/all_gather | solution.py:373
  404.9 6.4 %copy.98 = bf16[16384,128]{1,0:T(8,128)(2,1)} copy(bf16[16384,128]{0,1:T(8,128)(2,1)} %all-gather.11.cloned.1.call-done) | data formatting | bytes 8388608 | tf_op jit(solution)/shard_map/reshape | solution.py:374
  419.7 59.5 %reduce-scatter.11.cloned.1.call-done = f32[16,4096]{1,0:T(8,128)} async-done(((f32[256,4096]{1,0:T(8,128)}), f32[16,4096]{1,0:T(8,128)}) %reduce-scatter.11.cloned.1.call-update) | async-done | bytes 262160 | tf_op jit(solution)/shard_map/reduce_scatter | solution.py:368
  479.3 76.0 %reduce-scatter.7.cloned.1.call-done = f32[16,4096]{1,0:T(8,128)} async-done(((f32[256,4096]{1,0:T(8,128)}), f32[16,4096]{1,0:T(8,128)}) %reduce-scatter.7.cloned.1.call-update) | async-done | bytes 262160 | tf_op jit(solution)/shard_map/reduce_scatter | solution.py:368
  555.2 1.1 pad_maximum_fusion
  556.4 1.5 collective-permute-start.1
  559.5 3.3 collective-permute-done.1
  (96 shorter events, 22.5 us)
Async XLA Ops:
  7.2 267.7 %copy-start = (bf16[1,256,4096]{2,1,0:T(8,128)(2,1)S(1)}, bf16[1,256,4096]{2,1,0:T(8,128)(2,1)}, u32[]{:S(2)}) copy-start(bf16[1,256,4096]{2,1,0:T(8,128)(2,1)} %param.12) | copy-start | bytes 6291460
  7.2 56.9 %all-gather.5.cloned.1.call-start = ((), (), s32[]{:S(2)}) async-start(), calls=%async_computation.4 | async-start | bytes 4456448 | tf_op jit(solution)/shard_map/all_gather | solution.py:301
  10.3 100.5 %all-gather.9.cloned.1.call-start = ((), (), s32[]{:S(2)}) async-start(), calls=%async_computation.8 | async-start | bytes 2228224 | tf_op jit(solution)/shard_map/all_gather | solution.py:326
  70.8 116.3 %all-gather.7.cloned.1.call-start = ((), (), s32[]{:S(2)}) async-start(), calls=%async_computation.5 | async-start | bytes 2228224 | tf_op jit(solution)/shard_map/all_gather | solution.py:326
  71.5 201.9 %reduce-scatter.9.cloned.1.call-start = ((), (), s32[]{:S(2)}) async-start(), calls=%async_computation.9 | async-start | bytes 4456448 | tf_op jit(solution)/shard_map/reduce_scatter | solution.py:341
  110.8 1.6 copy-start.2
  187.0 152.0 %reduce-scatter.5.cloned.1.call-start = ((), (), s32[]{:S(2)}) async-start(), calls=%async_computation.6 | async-start | bytes 4456448 | tf_op jit(solution)/shard_map/reduce_scatter | solution.py:341
  187.1 1.6 copy-start.1
  262.8 1.2 copy-start.4
  262.8 142.1 %all-gather.11.cloned.1.call-start = ((), (), s32[]{:S(2)}) async-start(), calls=%async_computation.11 | async-start | bytes 4325376 | tf_op jit(solution)/shard_map/all_gather | solution.py:373
  264.0 6.9 %copy-start.7 = (bf16[2,16,1,16,128]{4,3,2,1,0:T(8,128)(2,1)S(1)}, bf16[2,16,1,16,128]{4,3,2,1,0:T(8,128)(2,1)}, u32[]{:S(2)}) copy-start(bf16[2,16,1,16,128]{4,3,2,1,0:T(8,128)(2,1)} %get-tuple-element.29) | copy-start | bytes 393220
  269.0 210.3 %reduce-scatter.11.cloned.1.call-start = ((), (), s32[]{:S(2)}) async-start(), calls=%async_computation.10 | async-start | bytes 4456448 | tf_op jit(solution)/shard_map/reduce_scatter | solution.py:368
  269.3 1.6 collective-permute-start
  271.0 1.4 copy-start.9
  274.9 2.8 copy-start.5
  274.9 2.8 copy-start.6
  277.7 277.6 %reduce-scatter.7.cloned.1.call-start = ((), (), s32[]{:S(2)}) async-start(), calls=%async_computation.7 | async-start | bytes 4456448 | tf_op jit(solution)/shard_map/reduce_scatter | solution.py:368
  340.4 2.8 copy-start.8
  367.5 188.9 %copy-start.3 = (bf16[1,32,4096]{2,1,0:T(8,128)(2,1)S(1)}, bf16[1,32,4096]{2,1,0:T(8,128)(2,1)}, u32[]{:S(2)}) copy-start(bf16[1,32,4096]{2,1,0:T(8,128)(2,1)} %param.8) | copy-start | bytes 786436
  556.4 6.4 %collective-permute-start.1 = (bf16[32,4096]{1,0:T(8,128)(2,1)S(1)}, bf16[32,4096]{1,0:T(8,128)(2,1)S(1)}, u32[]{:S(2)}, u32[]{:S(2)}) collective-permute-start(bf16[32,4096]{1,0:T(8,128)(2,1)S(1)} %fusion.25), channel_id=1, source_target_pairs={{16,0},{0,16},{17,1},{1,17},{18,2},{2,18},{19,3},{3,19},{20,4},{4,... | collective-permute-start | bytes 786440 | tf_op jit(solution)/shard_map/ppermute | solution.py:22
Sparse Core Ops, SparseCore 0:
  10.8 53.2 all-gather.4
  70.9 39.8 all-gather.8
  113.5 40.1 all-gather.6
  187.1 74.0 reduce-scatter.8
  265.3 73.5 reduce-scatter.4
  341.7 63.1 all-gather.10
  408.8 70.4 reduce-scatter.10
  483.6 71.5 reduce-scatter.6
where the time goes:
time: 571 us; the launch traced here: 570 us
  waiting for transfers between devices  328 us (57%)
  Pallas kernels  85.1 us (15%)
  blocking collectives  41.1 us (7%)
  between operations  37.8 us (7%)
  local copies, waits for them, and re-layouts  34.5 us (6%)
  other arithmetic  23.3 us (4%)
  matrix products  18 us (3%)
    reduce_scatter x2, waiting for transfers between devices, body(): lax.psum_scatter(product, 'tp', scatter_dimension=0, tiled=True)  136 us
    pallas_call x2, Pallas kernels, attend(): pl.pallas_call(lambda *refs: attend_kernel(*refs, tile=tile, scale=scale)...  85.1 us
    reduce_scatter x2, waiting for transfers between devices, body(): share = lax.psum_scatter(scaled, 'tp', scatter_dimension=0, tiled=True)  59.8 us
    all_gather x1, waiting for transfers between devices, body(): all_rows = lax.all_gather(normed, 'tp', axis=0, tiled=True)  51.2 us
    all_gather x2, blocking collectives, body(): lses = lax.all_gather(lse, 'tp', axis=0)  41.1 us
    all_gather x2, waiting for transfers between devices, body(): lax.all_gather(by_chunk[:, :, c].reshape(heads_here, part_rows, HD), 'tp'...  39.1 us
    all_gather x1, waiting for transfers between devices, body(): pages = lax.all_gather(part, ('section', 'tp'), axis=0, tiled=True)  37.4 us
    unnamed x34, local copies, waits for them, and re-layouts  13.9 us
  transfers between devices with their start and end apart: 10, of which 8 were waited for; matrix products, arithmetic and copies ran while one was open for 11% of the time, Pallas kernels for 15%

commit v1 on v0

--- a/solution.py
+++ b/solution.py
@@ -181,7 +181,7 @@
 
 
 NEG = -1e30
-CHUNKS = 2
+CHUNKS = 1
 ROW_TILE = 256
 TILES = 4
 
@@ -272,6 +272,170 @@
     )(count, q_all, local_cache)
 
 
+def places(tp_count):
+    me = lax.axis_index("tp")
+    zs = tp_count // 4
+    core, x, z = me % 2, (me // 2) % 2, me // 4
+
+    def at(step, flip_x, flip_core):
+        x_at = 1 - x if flip_x else x
+        core_at = 1 - core if flip_core else core
+        return ((z + step + zs) % zs) * 4 + x_at * 2 + core_at
+
+    return zs, at
+
+
+def greet(peers):
+    barrier = pltpu.get_barrier_semaphore()
+    for peer in peers:
+        pl.semaphore_signal(
+            barrier, inc=1, device_id={"tp": peer}, device_id_type=pl.DeviceIdType.MESH
+        )
+    pl.semaphore_wait(barrier, len(peers))
+
+
+def send(src, dst, send_sems, recv_sems, slot, peer):
+    return pltpu.make_async_remote_copy(
+        src_ref=src,
+        dst_ref=dst,
+        send_sem=send_sems.at[slot],
+        recv_sem=recv_sems.at[slot],
+        device_id={"tp": peer},
+        device_id_type=pl.DeviceIdType.MESH,
+    )
+
+
+def gather_kernel(own_ref, all_ref, send_sems, recv_sems, own_sem, *, tp_count):
+    zs, at = places(tp_count)
+    me = at(0, False, False)
+    x_peer, core_peer = at(0, True, False), at(0, False, True)
+    greet([x_peer, core_peer] + [at(k, False, False) for k in range(1, zs)])
+    first_x, first_core = zs - 1, 2 * zs - 1
+    started = {}
+
+    def put(src, block, slot, peer):
+        started[slot] = send(src, all_ref.at[block], send_sems, recv_sems, slot, peer)
+        started[slot].start()
+
+    keep = pltpu.make_async_copy(own_ref, all_ref.at[me], own_sem)
+    keep.start()
+    put(own_ref, me, first_x, x_peer)
+    for k in range(1, zs):
+        put(own_ref, me, k - 1, at(k, False, False))
+    put(own_ref, me, first_core, core_peer)
+    order = [1, zs - 1] + list(range(2, zs - 1))
+
+    def x_arrived(k):
+        block = at(-k, True, False)
+        started[first_x + k].wait_recv()
+        put(all_ref.at[block], block, first_core + zs + k, core_peer)
+
+    for k in order:
+        block = at(-k, False, False)
+        started[k - 1].wait_recv()
+        put(all_ref.at[block], block, first_x + k, x_peer)
+        put(all_ref.at[block], block, first_core + k, core_peer)
+        if k == order[0]:
+            x_arrived(0)
+    for k in order:
+        x_arrived(k)
+    for slot in range(first_core, first_core + 2 * zs):
+        started[slot].wait_recv()
+    for slot in range(first_core + 2 * zs):
+        started[slot].wait_send()
+    keep.wait()
+
+
+def gather_all(own, collective_id):
+    tp_count = lax.axis_size("tp")
+    copies = tp_count - 1
+    return pl.pallas_call(
+        lambda *refs: gather_kernel(*refs, tp_count=tp_count),
+        out_shape=jax.ShapeDtypeStruct((tp_count,) + own.shape, own.dtype),
+        in_specs=[pl.BlockSpec(memory_space=pl.ANY)],
+        out_specs=pl.BlockSpec(memory_space=pl.ANY),
+        scratch_shapes=[
+            pltpu.SemaphoreType.DMA((copies,)),
+            pltpu.SemaphoreType.DMA((copies,)),
+            pltpu.SemaphoreType.DMA,
+        ],
+        compiler_params=pltpu.CompilerParams(
+            collective_id=collective_id, has_side_effects=True
+        ),
+    )(own)
+
+
+def reduce_kernel(
+    parts_ref, sum_ref, core_in, x_out, x_in, z_out, z_in, send_sems, recv_sems, *, tp_count
+):
+    zs, at = places(tp_count)
+    x_peer, core_peer = at(0, True, False), at(0, False, True)
+    greet([x_peer, core_peer] + [at(k, False, False) for k in range(1, zs)])
+    order = list(range(1, zs)) + [0]
+    first_x, first_z = 2 * zs, 3 * zs
+    started = {}
+
+    def put(src, dst, slot, peer):
+        started[slot] = send(src, dst, send_sems, recv_sems, slot, peer)
+        started[slot].start()
+
+    for near in (0, 1):
+        for k in order:
+            slot = 2 * k + near
+            block = at(k, near == 0, True)
+            put(parts_ref.at[block], core_in.at[slot], slot, core_peer)
+
+    def pair_sum(k, near):
+        started[2 * k + near].wait_recv()
+        return parts_ref[at(k, near == 0, False)].astype(jnp.float32) + core_in[
+            2 * k + near
+        ].astype(jnp.float32)
+
+    for k in order:
+        x_out[k] = pair_sum(k, 0).astype(jnp.bfloat16)
+        put(x_out.at[k], x_in.at[k], first_x + k, x_peer)
+    for k in order:
+        total = pair_sum(k, 1)
+        started[first_x + k].wait_recv()
+        total = total + x_in[k].astype(jnp.float32)
+        if k:
+            z_out[k - 1] = total.astype(jnp.bfloat16)
+            put(z_out.at[k - 1], z_in.at[k - 1], first_z + k - 1, at(k, False, False))
+        else:
+            sum_ref[...] = total
+    for k in range(1, zs):
+        started[first_z + k - 1].wait_recv()
+        sum_ref[...] += z_in[k - 1].astype(jnp.float32)
+    for slot in range(4 * zs - 1):
+        started[slot].wait_send()
+
+
+def reduce_all(parts, collective_id):
+    tp_count, rows, cols = parts.shape
+    zs = tp_count // 4
+    copies = 4 * zs - 1
+    return pl.pallas_call(
+        lambda *refs: reduce_kernel(*refs, tp_count=tp_count),
+        out_shape=jax.ShapeDtypeStruct((rows, cols), jnp.float32),
+        in_specs=[pl.BlockSpec(memory_space=pltpu.VMEM)],
+        out_specs=pl.BlockSpec(memory_space=pltpu.VMEM),
+        scratch_shapes=[
+            pltpu.VMEM((2 * zs, rows, cols), jnp.bfloat16),
+            pltpu.VMEM((zs, rows, cols), jnp.bfloat16),
+            pltpu.VMEM((zs, rows, cols), jnp.bfloat16),
+            pltpu.VMEM((zs - 1, rows, cols), jnp.bfloat16),
+            pltpu.VMEM((zs - 1, rows, cols), jnp.bfloat16),
+            pltpu.SemaphoreType.DMA((copies,)),
+            pltpu.SemaphoreType.DMA((copies,)),
+        ],
+        compiler_params=pltpu.CompilerParams(
+            collective_id=collective_id,
+            has_side_effects=True,
+            vmem_limit_bytes=32 * 1024 * 1024,
+        ),
+    )(parts)
+
+
 def take_pages(pages, owner_flat, target, capacity):
     mine = owner_flat == target
     rank = jnp.cumsum(mine.astype(jnp.int32)) - 1
@@ -298,7 +462,7 @@
     scale = math.log2(math.e) / math.sqrt(HD)
     residual = hidden_in[0].astype(jnp.float32)
     normed = rms_norm(residual, attn_gain[0]).astype(jnp.bfloat16)
-    all_rows = lax.all_gather(normed, "tp", axis=0, tiled=True)
+    all_rows = gather_all(normed, 0).reshape(FRESH, D)
     block_start = starts[0]
     positions = block_start + jnp.arange(FRESH, dtype=jnp.int32)
     queries = jnp.dot(all_rows, w_query[0], preferred_element_type=jnp.float32)
@@ -323,9 +487,7 @@
     local_cache = cache[0]
     token = jnp.arange(FRESH, dtype=jnp.int32).reshape(tp_count, CHUNKS, step)
     gathered = [
-        lax.all_gather(
-            by_chunk[:, :, c].reshape(heads_here, part_rows, HD), "tp", axis=0, tiled=True
-        )
+        gather_all(by_chunk[:, :, c].reshape(heads_here * part_rows, HD), 1 + 4 * c)
         for c in range(CHUNKS)
     ]
     outs = []
@@ -334,11 +496,12 @@
         sums, lse = attend(q_all, local_cache, count)
         sums = sums.reshape(H, part_rows, HD)
         lse = lse.reshape(H, part_rows)
-        lses = lax.all_gather(lse, "tp", axis=0)
+        lses = gather_all(lse, 2 + 4 * c)
         peak = jnp.max(lses, axis=0)
         whole = peak + jnp.log2(jnp.sum(jnp.exp2(lses - peak[None]), axis=0))
         scaled = sums * jnp.exp2(lse - whole)[:, :, None]
-        share = lax.psum_scatter(scaled, "tp", scatter_dimension=0, tiled=True)
+        scaled = scaled.astype(jnp.bfloat16).reshape(tp_count, heads_here * part_rows, HD)
+        share = reduce_all(scaled, 3 + 4 * c).reshape(heads_here, part_rows, HD)
         whole_here = lax.dynamic_slice_in_dim(whole, tp_rank * heads_here, heads_here, 0)
         mine = by_chunk[:, :, c].reshape(heads_here, part_rows, HD)
         new_scores = jnp.einsum(
@@ -365,7 +528,8 @@
         attended = jnp.transpose(attended.astype(jnp.bfloat16), (1, 0, 2))
         attended = attended.reshape(part_rows, query_cols)
         product = jnp.dot(attended, w_out[0], preferred_element_type=jnp.float32)
-        outs.append(lax.psum_scatter(product, "tp", scatter_dimension=0, tiled=True))
+        product = product.astype(jnp.bfloat16).reshape(tp_count, step, D)
+        outs.append(reduce_all(product, 4 + 4 * c))
     projected_rows = jnp.stack(outs, axis=0).reshape(local_rows, D)
     layer_out = (residual + projected_rows).astype(jnp.bfloat16)
     passed_on = passed_along(layer_out, "section", 1)

time: 571 us -> 360 us (0.63)
  waiting for transfers between devices: 328 us -> 0.04 us
  Pallas kernels: 85.1 us -> 265 us
  blocking collectives: 41.1 us -> 0 us
  local copies, waits for them, and re-layouts: 34.5 us -> 21.7 us
  matrix products: 18 us -> 11.6 us
    reduce_scatter x4 -> x0, waiting for transfers between devices: 195 us -> none  [the longest x2 136 us: body(): lax.psum_scatter(product, 'tp', scatter_dimension=0, tiled=True)]
    pallas_call x0 -> x5, Pallas kernels: none -> 182 us  [the longest x3 112 us: gather_all(): pl.pallas_call(lambda *refs: gather_kernel(*refs, tp_count=tp_count), out...]
    all_gather x3 -> x0, waiting for transfers between devices: 90.3 us -> none  [the longest x1 51.2 us: body(): all_rows = lax.all_gather(normed, 'tp', axis=0, tiled=True)]
    all_gather x2 -> x0, blocking collectives: 41.1 us -> none  [body(): lses = lax.all_gather(lse, 'tp', axis=0)]
    all_gather x1, waiting for transfers between devices: 37.4 us -> 0.02 us  [body(): pages = lax.all_gather(part, ('section', 'tp'), axis=0, tiled=True)]
    reshape x2 -> x1, local copies, waits for them, and re-layouts: 11.3 us -> 0.99 us  [body(): share = reduce_all(scaled, 3 + 4 * c).reshape(heads_here, part_rows, HD)]
    mul x2 -> x0, other arithmetic: 9.42 us -> none  [body(): scaled = sums * jnp.exp2(lse - whole)[:, :, None]]
    convert_element_type x0 -> x1, other arithmetic: none -> 7.64 us  [body(): scaled.astype(jnp.bfloat16).reshape(tp_count, heads_here * part_rows, HD)]
  transfers between devices with their start and end apart: 10 -> 3, of which waited for: 8 -> 0; matrix products, arithmetic and copies ran while one was open for 11% -> 8% of each run, Pallas kernels for 15% -> 64%
where the time goes in v1:
time: 360 us; the launch traced here: 359 us
  Pallas kernels  265 us (74%)
  between operations  37.6 us (10%)
  other arithmetic  22.5 us (6%)
  local copies, waits for them, and re-layouts  21.7 us (6%)
  matrix products  11.6 us (3%)
    pallas_call x3, Pallas kernels, gather_all(): pl.pallas_call(lambda *refs: gather_kernel(*refs, tp_count=tp_count), out...  112 us
    pallas_call x1, Pallas kernels, attend(): pl.pallas_call(lambda *refs: attend_kernel(*refs, tile=tile, scale=scale)...  83 us
    pallas_call x2, Pallas kernels, reduce_all(): pl.pallas_call(lambda *refs: reduce_kernel(*refs, tp_count=tp_count), out...  69.6 us
    unnamed x28, local copies, waits for them, and re-layouts  11.7 us
    convert_element_type x1, other arithmetic, body(): scaled.astype(jnp.bfloat16).reshape(tp_count, heads_here * part_rows, HD)  7.64 us
  transfers between devices with their start and end apart: 3, of which 0 were waited for; matrix products, arithmetic and copies ran while one was open for 8% of the time, Pallas kernels for 64%

profile of v1, /device:TPU:0, one launch (start us, length us, event | category | flops | bytes accessed | tf_op | source)
XLA Modules:
  0.0 358.8 jit_solution(2064398234571899499)
XLA Ops:
  7.2 1.2 fusion.18
  8.5 1.8 fusion.20.refs_0_
  10.3 34.3 %shard_map.95 = bf16[16,32,4096]{2,1,0:T(8,128)(2,1)} custom-call(bf16[32,4096]{1,0:T(8,128)(2,1)} %fusion.20.refs_0_), custom_call_target="tpu_custom_call" | custom-call | tf_op jit(solution)/shard_map/pallas_call | solution.py:352
  45.2 3.7 %bitcast_convert_fusion = (f32[512,1,128]{0,2,1:T(8,128)S(1)}, bf16[512,128]{0,1:T(8,128)(2,1)S(1)}) fusion(bf16[512,4096]{1,0:T(8,128)(2,1)} %bitcast.75, bf16[1,4096,128]{2,1,0:T(8,128)(2,1)S(1)} %copy-done.4), kind=kOutput, calls=%fused_computation.52 | convolution fusion | flops 537001984 | bytes 5636096 | tf_op jit(solution)/shard_map/dot_general | solution.py:472
  50.6 1.8 multiply_cosine_fusion
  52.4 4.2 %fusion.9 = bf16[512,256]{0,1:T(8,128)(2,1)S(1)} fusion(bf16[512,4096]{1,0:T(8,128)(2,1)} %bitcast.76, bf16[1,4096,256]{2,1,0:T(8,128)(2,1)} %param.10), kind=kOutput, calls=%fused_computation.14 | convolution fusion | flops 1073872896 | bytes 6553600 | tf_op jit(solution)/shard_map/dot_general | solution.py:468
  57.1 1.9 subtract_convert_fusion
  58.9 1.8 pad_maximum_fusion
  60.7 44.4 %shard_map.96 = bf16[16,1024,128]{2,1,0:T(8,128)(2,1)} custom-call(bf16[1024,128]{1,0:T(8,128)(2,1)} %bitcast.91), custom_call_target="tpu_custom_call" | custom-call | tf_op jit(solution)/shard_map/pallas_call | solution.py:352
  105.2 83.0 %shard_map.97 = (f32[8,2048,128]{2,1,0:T(8,128)}, f32[8,1,2048]{2,1,0:T(1,128)S(1)}) custom-call(s32[1]{0:T(128)} %bitcast.2.refs_0_, bf16[8,2048,128]{2,1,0:T(8,128)(2,1)} %bitcast.90, bf16[8,4096,256]{2,1,0:T(8,128)(2,1)} %bitcast.96), custom_call_target="tpu_custom_call" | custom-call | flops 34359738368 | bytes 29360128 | tf_op jit(solution)/shard_map/pallas_call | solution.py:248
  189.0 33.4 %shard_map.98 = f32[16,32,512]{2,1,0:T(8,128)} custom-call(f32[32,512]{1,0:T(8,128)} %reshape.316.refs_0_), custom_call_target="tpu_custom_call" | custom-call | tf_op jit(solution)/shard_map/pallas_call | solution.py:352
  222.4 1.3 reduce_max.18
  223.7 1.4 exponential_reduce_fusion
  225.4 7.6 %multiply_convert_fusion.refs_0_ = bf16[16,1024,128]{2,1,0:T(8,128)(2,1)} fusion(f32[16,1024,128]{2,1,0:T(8,128)} %bitcast.77, f32[16,1024]{1,0:T(8,128)S(1)} %multiply_exponential_fusion.1), kind=kLoop, calls=%fused_computation | loop fusion | flops 4194304 | bytes 12648448 | tf_op jit(solution)/shard_map/convert_element_type | solution.py:503
  233.1 2.2 copy-done.1
  235.3 33.4 %shard_map.99 = f32[1024,128]{1,0:T(8,128)S(1)} custom-call(bf16[16,1024,128]{2,1,0:T(8,128)(2,1)S(1)} %copy-done.1), custom_call_target="tpu_custom_call" | custom-call | tf_op jit(solution)/shard_map/pallas_call | solution.py:417
  268.6 1.0 copy.53
  270.4 1.6 fusion.3
  272.6 0.9 fusion.8
  273.5 1.3 convolution_convert_fusion
  274.8 36.3 %shard_map.100 = f32[32,4096]{1,0:T(8,128)S(1)} custom-call(bf16[16,32,4096]{2,1,0:T(8,128)(2,1)S(1)} %bitcast.73), custom_call_target="tpu_custom_call" | custom-call | tf_op jit(solution)/shard_map/pallas_call | solution.py:417
  334.8 6.4 %copy.73 = bf16[16384,128]{1,0:T(8,128)(2,1)} copy(bf16[16384,128]{0,1:T(8,128)(2,1)} %all-gather.2.cloned.1.call-done) | data formatting | bytes 8388608 | tf_op jit(solution)/shard_map/reshape | solution.py:538
  341.9 0.8 dynamic-slice_dynamic-update-slice_fusion.10
  342.7 0.8 dynamic-slice_dynamic-update-slice_fusion.9
  343.5 0.8 dynamic-slice_dynamic-update-slice_fusion.8
  344.2 0.8 dynamic-slice_dynamic-update-slice_fusion.7
  345.0 0.8 dynamic-slice_dynamic-update-slice_fusion.6
  345.8 0.8 dynamic-slice_dynamic-update-slice_fusion.5
  346.5 0.8 dynamic-slice_dynamic-update-slice_fusion.4
  348.8 0.8 dynamic-slice_dynamic-update-slice_fusion.1
  349.6 0.8 dynamic-slice_dynamic-update-slice_fusion
  350.4 0.8 broadcast_select_fusion
  (53 shorter events, 8.7 us)
Async XLA Ops:
  7.2 266.3 %copy-start = (bf16[1,256,4096]{2,1,0:T(8,128)(2,1)S(1)}, bf16[1,256,4096]{2,1,0:T(8,128)(2,1)}, u32[]{:S(2)}) copy-start(bf16[1,256,4096]{2,1,0:T(8,128)(2,1)} %param.12) | copy-start | bytes 6291460
  7.2 327.6 %all-gather.2.cloned.1.call-start = ((), (), s32[]{:S(2)}) async-start(), calls=%async_computation | async-start | bytes 4325376 | tf_op jit(solution)/shard_map/all_gather | solution.py:537
  10.3 34.9 %copy-start.4 = (bf16[1,4096,128]{2,1,0:T(8,128)(2,1)S(1)}, bf16[1,4096,128]{2,1,0:T(8,128)(2,1)}, u32[]{:S(2)}) copy-start(bf16[1,4096,128]{2,1,0:T(8,128)(2,1)} %param.11) | copy-start | bytes 3145732
  50.2 220.2 %collective-permute-start = (bf16[512,128]{0,1:T(8,128)(2,1)}, bf16[512,128]{0,1:T(8,128)(2,1)S(1)}, u32[]{:S(2)}, u32[]{:S(2)}) collective-permute-start(bf16[512,128]{0,1:T(8,128)(2,1)} %fusion.32), channel_id=1, source_target_pairs={{0,1},{1,0},{2,3},{3,2},{4,5},{5,4},{6,7},{7,6},{8,9},{9,8},{10,11... | collective-permute-start | bytes 393224 | tf_op jit(solution)/shard_map/ppermute | solution.py:478
  225.4 7.7 %copy-start.6 = (s32[2,8,2,4]{1,3,2,0:T(4,128)S(1)}, s32[2,8,2,4]{1,3,2,0:T(4,128)}, u32[]{:S(2)}) copy-start(s32[2,8,2,4]{1,3,2,0:T(4,128)} %param.15) | copy-start | bytes 1540
  233.1 2.2 copy-start.1
  235.3 35.1 %copy-start.2 = (bf16[512,2,128]{2,0,1:T(8,128)(2,1)S(1)}, bf16[512,2,128]{2,0,1:T(8,128)(2,1)}, u32[]{:S(2)}) copy-start(bf16[512,2,128]{2,0,1:T(8,128)(2,1)} %pad_maximum_fusion) | copy-start | bytes 786436
  270.4 2.2 copy-start.5
  274.8 36.3 %copy-start.3 = (bf16[1,32,4096]{2,1,0:T(8,128)(2,1)S(1)}, bf16[1,32,4096]{2,1,0:T(8,128)(2,1)}, u32[]{:S(2)}) copy-start(bf16[1,32,4096]{2,1,0:T(8,128)(2,1)} %param.8) | copy-start | bytes 786436
  311.1 23.6 %collective-permute-start.1 = (bf16[32,4096]{1,0:T(8,128)(2,1)S(1)}, bf16[32,4096]{1,0:T(8,128)(2,1)S(1)}, u32[]{:S(2)}, u32[]{:S(2)}) collective-permute-start(bf16[32,4096]{1,0:T(8,128)(2,1)S(1)} %fusion.21), channel_id=1, source_target_pairs={{16,0},{0,16},{17,1},{1,17},{18,2},{2,18},{19,3},{3,19},{20,4},{4,... | collective-permute-start | bytes 786440 | tf_op jit(solution)/shard_map/ppermute | solution.py:22
Sparse Core Ops, SparseCore 0:
  50.7 81.3 all-gather.1

commit v2 on v1

--- a/solution.py
+++ b/solution.py
@@ -436,14 +436,34 @@
     )(parts)
 
 
+def page_kernel(picks_ref, fills_ref, page_ref, slot_ref):
+    keep = fills_ref[pl.program_id(0)] > 0
+
+    @pl.when(keep)
+    def _():
+        slot_ref[...] = page_ref[...]
+
+    @pl.when(jnp.logical_not(keep))
+    def _():
+        slot_ref[...] = jnp.zeros_like(slot_ref)
+
+
 def take_pages(pages, owner_flat, target, capacity):
     mine = owner_flat == target
     rank = jnp.cumsum(mine.astype(jnp.int32)) - 1
     wanted = mine[None, :] & (rank[None, :] == jnp.arange(capacity)[:, None])
     picked = jnp.sum(jnp.where(wanted, jnp.arange(mine.shape[0])[None, :], 0), axis=1)
-    filled = jnp.any(wanted, axis=1)
-    taken = [lax.dynamic_index_in_dim(pages, picked[k], 0, True) for k in range(capacity)]
-    return jnp.where(filled[:, None, None], jnp.concatenate(taken, axis=0), 0)
+    filled = jnp.any(wanted, axis=1).astype(jnp.int32)
+    return pl.pallas_call(
+        page_kernel,
+        grid_spec=pltpu.PrefetchScalarGridSpec(
+            num_scalar_prefetch=2,
+            grid=(capacity,),
+            in_specs=[pl.BlockSpec((1, PAGE, HD), lambda k, picks, fills: (picks[k], 0, 0))],
+            out_specs=pl.BlockSpec((1, PAGE, HD), lambda k, picks, fills: (k, 0, 0)),
+        ),
+        out_shape=jax.ShapeDtypeStruct((capacity, PAGE, HD), pages.dtype),
+    )(picked, filled, pages)
 
 
 def body(hidden_in, attn_gain, w_query, w_keyval, w_out, cache, starts, owners):
@@ -534,6 +554,7 @@
     layer_out = (residual + projected_rows).astype(jnp.bfloat16)
     passed_on = passed_along(layer_out, "section", 1)
 
+    part, _ = lax.optimization_barrier((part, gathered[0]))
     pages = lax.all_gather(part, ("section", "tp"), axis=0, tiled=True)
     pages = pages.reshape(-1, PAGE, HD)
     owner_flat = owners.reshape(-1)

time: 360 us -> 326 us (0.906)
  between operations: 37.6 us -> 15.2 us
  local copies, waits for them, and re-layouts: 21.7 us -> 9.46 us
  waiting for transfers between devices: 0.04 us -> 5.39 us
    unnamed x28 -> x25, local copies, waits for them, and re-layouts: 11.7 us -> 1.72 us
    pallas_call x3, Pallas kernels: 112 us -> 103 us  [gather_all(): pl.pallas_call(lambda *refs: gather_kernel(*refs, tp_count=tp_count), out...]
    reshape x1 -> x0, local copies, waits for them, and re-layouts: 6.4 us -> none  [body(): pages = pages.reshape(-1, PAGE, HD)]
    all_gather x0 -> x1, local copies, waits for them, and re-layouts: none -> 6.39 us  [body(): pages = lax.all_gather(part, ('section', 'tp'), axis=0, tiled=True)]
    pallas_call x0 -> x1, Pallas kernels: none -> 6.08 us  [take_pages(): pl.pallas_call(page_kernel, grid_spec=pltpu.PrefetchScalarGridSpec(num_sc...]
    ppermute x1, waiting for transfers between devices: 0.01 us -> 5.37 us  [passed_along(): return lax.ppermute(block, axis, route)]
  transfers between devices with their start and end apart: 3 -> 3, of which waited for: 0 -> 1; matrix products, arithmetic and copies ran while one was open for 8% -> 5% of each run, Pallas kernels for 64% -> 56%
where the time goes in v2:
time: 326 us; the launch traced here: 323 us
  Pallas kernels  263 us (81%)
  other arithmetic  20.5 us (6%)
  between operations  15.2 us (5%)
  local copies, waits for them, and re-layouts  9.46 us (3%)
  matrix products  9.44 us (3%)
  waiting for transfers between devices  5.39 us (2%)
    pallas_call x3, Pallas kernels, gather_all(): pl.pallas_call(lambda *refs: gather_kernel(*refs, tp_count=tp_count), out...  103 us
    pallas_call x1, Pallas kernels, attend(): pl.pallas_call(lambda *refs: attend_kernel(*refs, tile=tile, scale=scale)...  82.8 us
    pallas_call x2, Pallas kernels, reduce_all(): pl.pallas_call(lambda *refs: reduce_kernel(*refs, tp_count=tp_count), out...  70.8 us
  transfers between devices with their start and end apart: 3, of which 1 were waited for; matrix products, arithmetic and copies ran while one was open for 5% of the time, Pallas kernels for 56%

profile of v2, /device:TPU:0, one launch (start us, length us, event | category | flops | bytes accessed | tf_op | source)
XLA Modules:
  0.0 323.1 jit_solution(579063090829907161)
XLA Ops:
  8.0 1.1 fusion.18
  9.2 1.8 fusion.20.refs_0_
  11.0 34.3 %shard_map.95 = bf16[16,32,4096]{2,1,0:T(8,128)(2,1)} custom-call(bf16[32,4096]{1,0:T(8,128)(2,1)} %fusion.20.refs_0_), custom_call_target="tpu_custom_call" | custom-call | tf_op jit(solution)/shard_map/pallas_call | solution.py:352
  45.2 4.3 %fusion.9 = bf16[512,256]{0,1:T(8,128)(2,1)S(1)} fusion(bf16[512,4096]{1,0:T(8,128)(2,1)} %bitcast.63, bf16[1,4096,256]{2,1,0:T(8,128)(2,1)} %param.10), kind=kOutput, calls=%fused_computation.14 | convolution fusion | flops 1073872896 | bytes 6553600 | tf_op jit(solution)/shard_map/dot_general | solution.py:488
  49.6 1.5 bitcast_convert_fusion
  51.1 1.8 multiply_cosine_fusion
  52.9 1.2 fusion.29
  54.6 1.2 subtract_convert_fusion
  55.8 0.9 pad_maximum_fusion
  56.6 40.1 %shard_map.96 = bf16[16,1024,128]{2,1,0:T(8,128)(2,1)} custom-call(bf16[1024,128]{1,0:T(8,128)(2,1)} %bitcast.68), custom_call_target="tpu_custom_call" | custom-call | tf_op jit(solution)/shard_map/pallas_call | solution.py:352
  96.8 0.7 fusion.32
  98.0 82.8 %shard_map.97 = (f32[8,2048,128]{2,1,0:T(8,128)}, f32[8,1,2048]{2,1,0:T(1,128)S(1)}) custom-call(s32[1]{0:T(128)} %bitcast.2.refs_0_, bf16[8,2048,128]{2,1,0:T(8,128)(2,1)} %bitcast.67, bf16[8,4096,256]{2,1,0:T(8,128)(2,1)} %bitcast.73), custom_call_target="tpu_custom_call" | custom-call | flops 34359738368 | bytes 29360128 | tf_op jit(solution)/shard_map/pallas_call | solution.py:248
  180.9 0.6 reshape.315.refs_0_
  181.8 0.8 reduce-window.8
  182.6 28.5 %shard_map.98 = f32[16,32,512]{2,1,0:T(8,128)} custom-call(f32[32,512]{1,0:T(8,128)} %reshape.315.refs_0_), custom_call_target="tpu_custom_call" | custom-call | tf_op jit(solution)/shard_map/pallas_call | solution.py:352
  211.0 1.3 reduce_max.18
  212.3 1.4 exponential_reduce_fusion
  213.9 0.5 copy-done.6
  214.4 5.2 %multiply_convert_fusion.refs_0_ = bf16[16,1024,128]{2,1,0:T(8,128)(2,1)S(1)} fusion(f32[16,1024,128]{2,1,0:T(8,128)} %bitcast.66, f32[16,1024]{1,0:T(8,128)S(1)} %multiply_exponential_fusion.1), kind=kLoop, calls=%fused_computation | loop fusion | flops 4194304 | bytes 12648448 | tf_op jit(solution)/shard_map/convert_element_type | solution.py:523
  219.7 35.8 %shard_map.99 = f32[1024,128]{1,0:T(8,128)S(1)} custom-call(bf16[16,1024,128]{2,1,0:T(8,128)(2,1)S(1)} %multiply_convert_fusion.refs_0_), custom_call_target="tpu_custom_call" | custom-call | tf_op jit(solution)/shard_map/pallas_call | solution.py:417
  256.0 0.6 fusion.3
  256.6 0.6 fusion.4
  257.1 0.7 multiply_add_fusion.1
  257.9 1.7 fusion.8
  259.6 1.3 convolution_convert_fusion
  261.0 35.0 %shard_map.100 = f32[32,4096]{1,0:T(8,128)S(1)} custom-call(bf16[16,32,4096]{2,1,0:T(8,128)(2,1)S(1)} %bitcast.61), custom_call_target="tpu_custom_call" | custom-call | tf_op jit(solution)/shard_map/pallas_call | solution.py:417
  296.6 0.5 convert_element_type.89.fills_ref
  297.1 0.6 select_reduce_fusion.picks_ref
  297.7 5.4 %collective-permute-done.1 = bf16[32,4096]{1,0:T(8,128)(2,1)S(1)} collective-permute-done((bf16[32,4096]{1,0:T(8,128)(2,1)S(1)}, bf16[32,4096]{1,0:T(8,128)(2,1)S(1)}, u32[]{:S(2)}, u32[]{:S(2)}) %collective-permute-start.1) | collective-permute-done | bytes 262176 | tf_op jit(solution)/shard_map/ppermute | solution.py:22
  303.1 6.4 %copy.36 = bf16[16384,128]{1,0:T(8,128)(2,1)} copy(bf16[16384,128]{0,1:T(8,128)(2,1)} %all-gather.2.cloned.1.call-done) | data formatting | bytes 8388608 | tf_op jit(solution)/shard_map/all_gather | solution.py:558
  309.5 6.1 %shard_map.101 = bf16[12,128,128]{2,1,0:T(8,128)(2,1)} custom-call(s32[12]{0:T(128)} %select_reduce_fusion.picks_ref, s32[12]{0:T(128)} %convert_element_type.89.fills_ref, bf16[128,128,128]{2,1,0:T(8,128)(2,1)} %bitcast.65), custom_call_target="tpu_custom_call" | custom-call | tf_op jit(solution)/shard_map/pallas_call | solution.py:457
  315.6 0.7 copy.44
  (49 shorter events, 2.5 us)
Async XLA Ops:
  7.2 252.5 %copy-start = (bf16[1,256,4096]{2,1,0:T(8,128)(2,1)S(1)}, bf16[1,256,4096]{2,1,0:T(8,128)(2,1)}, u32[]{:S(2)}) copy-start(bf16[1,256,4096]{2,1,0:T(8,128)(2,1)} %param.12) | copy-start | bytes 6291460
  7.2 295.9 %all-gather.2.cloned.1.call-start = ((), (), s32[]{:S(2)}) async-start(), calls=%async_computation | async-start | bytes 4325376 | tf_op jit(solution)/shard_map/all_gather | solution.py:558
  45.2 4.3 %copy-start.1 = (bf16[16,32,4096]{2,1,0:T(8,128)(2,1)S(1)}, bf16[16,32,4096]{2,1,0:T(8,128)(2,1)}, u32[]{:S(2)}) copy-start(bf16[16,32,4096]{2,1,0:T(8,128)(2,1)} %shard_map.95) | copy-start | bytes 12582916
  45.2 4.3 %copy-start.5 = (bf16[1,4096,128]{2,1,0:T(8,128)(2,1)S(1)}, bf16[1,4096,128]{2,1,0:T(8,128)(2,1)}, u32[]{:S(2)}) copy-start(bf16[1,4096,128]{2,1,0:T(8,128)(2,1)} %param.11) | copy-start | bytes 3145732
  56.6 40.1 %copy-start.8 = (bf16[512,1,64]{0,2,1:T(8,128)(2,1)S(1)}, bf16[512,1,64]{0,2,1:T(8,128)(2,1)}, u32[]{:S(2)}) copy-start(bf16[512,1,64]{0,2,1:T(8,128)(2,1)} %get-tuple-element.15) | copy-start | bytes 196612
  56.6 40.2 %copy-start.9 = (bf16[512,1,64]{0,2,1:T(8,128)(2,1)S(1)}, bf16[512,1,64]{0,2,1:T(8,128)(2,1)}, u32[]{:S(2)}) copy-start(bf16[512,1,64]{0,2,1:T(8,128)(2,1)} %get-tuple-element.16) | copy-start | bytes 196612
  97.5 158.4 %collective-permute-start = (bf16[512,128]{0,1:T(8,128)(2,1)}, bf16[512,128]{0,1:T(8,128)(2,1)}, u32[]{:S(2)}, u32[]{:S(2)}) collective-permute-start(bf16[512,128]{0,1:T(8,128)(2,1)} %fusion.32), channel_id=1, source_target_pairs={{0,1},{1,0},{2,3},{3,2},{4,5},{5,4},{6,7},{7,6},{8,9},{9,8},{10,11... | collective-permute-start | bytes 393224 | tf_op jit(solution)/shard_map/ppermute | solution.py:498
  97.9 83.6 %copy-start.10 = (s32[2,8,2,4]{1,3,2,0:T(4,128)S(1)}, s32[2,8,2,4]{1,3,2,0:T(4,128)}, u32[]{:S(2)}) copy-start(s32[2,8,2,4]{1,3,2,0:T(4,128)} %param.15) | copy-start | bytes 1540
  213.8 0.6 copy-start.6
  219.7 36.3 %copy-start.2 = (bf16[512,2,128]{2,0,1:T(8,128)(2,1)S(1)}, bf16[512,2,128]{2,0,1:T(8,128)(2,1)}, u32[]{:S(2)}) copy-start(bf16[512,2,128]{2,0,1:T(8,128)(2,1)} %pad_maximum_fusion) | copy-start | bytes 786436
  219.7 36.3 %copy-start.4 = (bf16[512,128]{0,1:T(8,128)(2,1)S(1)}, bf16[512,128]{0,1:T(8,128)(2,1)}, u32[]{:S(2)}) copy-start(bf16[512,128]{0,1:T(8,128)(2,1)} %fusion.32) | copy-start | bytes 393220
  260.9 35.0 %copy-start.3 = (bf16[1,32,4096]{2,1,0:T(8,128)(2,1)S(1)}, bf16[1,32,4096]{2,1,0:T(8,128)(2,1)}, u32[]{:S(2)}) copy-start(bf16[1,32,4096]{2,1,0:T(8,128)(2,1)} %param.8) | copy-start | bytes 786436
  260.9 35.1 %copy-start.7 = (s32[128,1]{1,0:T(8,128)S(1)}, s32[128,1]{1,0:T(8,128)}, u32[]{:S(2)}) copy-start(s32[128,1]{1,0:T(8,128)} %reduce-window.8) | copy-start | bytes 1540
  296.0 7.1 %collective-permute-start.1 = (bf16[32,4096]{1,0:T(8,128)(2,1)S(1)}, bf16[32,4096]{1,0:T(8,128)(2,1)S(1)}, u32[]{:S(2)}, u32[]{:S(2)}) collective-permute-start(bf16[32,4096]{1,0:T(8,128)(2,1)S(1)} %fusion.21), channel_id=1, source_target_pairs={{16,0},{0,16},{17,1},{1,17},{18,2},{2,18},{19,3},{3,19},{20,4},{4,... | collective-permute-start | bytes 786440 | tf_op jit(solution)/shard_map/ppermute | solution.py:22
Sparse Core Ops, SparseCore 0:
  97.6 72.3 all-gather.1
